TPU v7x, 512 devices: a whole 4x8x8 slice. The times are simulated.
512 devices in a mesh: leaf: 16 (over y, core), row: 8 (over z), col: 4 (over x).
Axes of the slice: x: 4, y: 8, z: 8, core: 2. Of those that a mesh axis runs over, the one named last changes fastest.
Arguments:
- rhs_leafs: bfloat16 [16384, 256], P(('leaf', 'row', 'col')), may hold values from -6 to 6
- rhs_mid: bfloat16 [16384, 256], P(('leaf', 'row', 'col')), may hold values from -6 to 6
- rhs_root: bfloat16 [16384, 256], P(('leaf', 'row', 'col')), may hold values from -6 to 6
- inv_leafs: bfloat16 [16384, 32, 128], P('leaf', ('row', 'col')), may hold values from -0.09375 to 0.09375
- inv_mid: bfloat16 [16384, 32, 256], P('leaf', ('row', 'col')), may hold values from -0.0625 to 0.0625
- inv_root: bfloat16 [16384, 32, 512], P('leaf', ('row', 'col')), may hold values from -0.046875 to 0.046875
- off_leafs: bfloat16 [8192, 32, 128], P('leaf', ('row', 'col')), may hold values from -0.09375 to 0.09375
- off_mid: bfloat16 [8192, 32, 256], P('leaf', ('row', 'col')), may hold values from -0.0625 to 0.0625
- owner_leafs: int32 [8192, 1], P('leaf'), may hold values from 0 to 31; in each aligned block of 512 rows (0 to 511, 512 to 1023, ...) at most 32 rows name the same one
- offset_leafs: int32 [8192], P('leaf'), may hold values from 0 to 63
- owner_mid: int32 [8192, 1], P('leaf'), may hold values from 0 to 31; in each aligned block of 512 rows (0 to 511, 512 to 1023, ...) at most 32 rows name the same one
- offset_mid: int32 [8192], P('leaf'), may hold values from 0 to 31
Outputs:
- solution_leafs: bfloat16 [16384, 256], P(('leaf', 'row', 'col'))
- solution_mid: bfloat16 [16384, 256], P(('leaf', 'row', 'col'))
- solution_root: bfloat16 [16384, 256], P(('leaf', 'row', 'col'))
Inputs may be any that keep to these rules, and one draw needn't show every extreme that they name: `owner_leafs`: in each leaf group's block of 512 rows no device is named more than 32 times, and some device is named exactly 32 times. `owner_mid`: in each leaf group's block of 512 rows no device is named more than 32 times, and some device is named exactly 32 times.
All inputs are finite; a program needn't handle non-finite values.
Results may differ from a plain program's by a relative error of at most 0.033.
Values may be sent and summed in bfloat16 or wider, within the bound.
A program may use at most 64 MiB of HBM per device.

v0:
```python
import jax
import jax.numpy as jnp
from jax import lax
from jax.sharding import PartitionSpec as P

CAP = 32


HIGHEST = lax.Precision.HIGHEST
CONTRACT_ROWS = (((0,), (0,)), ((), ()))


def partner_2(block, axis, apart):
    count = lax.axis_size(axis)
    route = []
    for low in range(count):
        high = low | 1 << apart
        if high != low and high < count:
            route += [(low, high), (high, low)]
    return lax.ppermute(block, axis, route)


def leaf_bit(leaf_index, bit_number):
    return leaf_index // (1 << bit_number) % 2


def group_gather(shard_rows, group_bits):
    leaf_index = lax.axis_index("leaf")
    joined = shard_rows
    for bit_number in range(group_bits):
        partner = partner_2(joined, "leaf", bit_number)
        is_upper = leaf_bit(leaf_index, bit_number) == 1
        joined = jnp.where(
            is_upper, jnp.concatenate([partner, joined], 0), jnp.concatenate([joined, partner], 0)
        )
    return joined


def group_sum(partial_value, group_bits):
    leaf_index = lax.axis_index("leaf")
    current = partial_value
    for bit_number in reversed(range(group_bits)):
        half_rows = current.shape[0] // 2
        lower_half = current[:half_rows]
        upper_half = current[half_rows:]
        is_upper = leaf_bit(leaf_index, bit_number) == 1
        outgoing = jnp.where(is_upper, lower_half, upper_half)
        kept_half = jnp.where(is_upper, upper_half, lower_half)
        current = kept_half + partner_2(outgoing.astype(jnp.bfloat16), "leaf", bit_number).astype(
            outgoing.dtype
        )
    return current


def flat_panel(inverse):
    return inverse.reshape(inverse.shape[0], inverse.shape[2])


def reduce_rows(panels, gathered):
    return lax.psum_scatter(
        jnp.dot(panels, gathered, preferred_element_type=jnp.float32).astype(jnp.bfloat16),
        ("row", "col"),
        scatter_dimension=0,
        tiled=True,
    )


def transpose_block(panels, column_rows):
    return lax.dot_general(
        panels,
        lax.all_gather(column_rows, ("row", "col"), axis=0, tiled=True),
        CONTRACT_ROWS,
        preferred_element_type=jnp.float32,
    )


def pick_rows(ancestor, owner_ids, offset):
    gathered = lax.all_gather(ancestor, ("row", "col"), axis=0, tiled=True)
    target = owner_ids[:, 0] * ancestor.shape[0] + offset
    return jnp.take(gathered, target, axis=0)


def route_update(off_panel, owner_ids, offset, level_rows, group_bits, target_count):
    gathered = group_gather(level_rows, group_bits)
    products = jnp.dot(flat_panel(off_panel), gathered, preferred_element_type=jnp.float32)
    owner_list = owner_ids[:, 0]
    block_count = lax.axis_size(("row", "col"))
    own_block = lax.axis_index(("row", "col"))
    is_mine = (owner_list == own_block).astype(jnp.float32)
    placement = (offset[:, None] == jnp.arange(target_count)[None, :]).astype(
        jnp.float32
    ) * is_mine[:, None]
    owner_hot = (owner_list[:, None] == jnp.arange(block_count)[None, :]).astype(jnp.int32)
    slot_rank = jnp.sum((jnp.cumsum(owner_hot, 0) - owner_hot) * owner_hot, 1)
    slot_index = owner_list * CAP + slot_rank
    slot_count = block_count * CAP
    row_of_slot = (
        jnp.zeros((slot_count,), jnp.int32)
        .at[slot_index]
        .set(jnp.arange(owner_list.shape[0], dtype=jnp.int32))
    )
    slot_filled = jnp.zeros((slot_count,), jnp.float32).at[slot_index].set(1.0)
    outgoing = (jnp.take(products, row_of_slot, axis=0) * slot_filled[:, None]).reshape(
        block_count, CAP, products.shape[1]
    )
    arrived = lax.all_to_all(
        outgoing.astype(jnp.bfloat16), ("row", "col"), split_axis=0, concat_axis=0, tiled=True
    ).astype(outgoing.dtype)
    slot_total = jnp.sum(arrived, 0)
    slot_hot = (slot_rank[:, None] == jnp.arange(CAP)[None, :]).astype(jnp.float32)
    layout = lax.dot_general(
        placement, slot_hot, CONTRACT_ROWS, precision=HIGHEST, preferred_element_type=jnp.float32
    )
    return jnp.dot(layout, slot_total, precision=HIGHEST, preferred_element_type=jnp.float32)


def shards(
    rhs_leafs,
    rhs_mid,
    rhs_root,
    inv_leafs,
    inv_mid,
    inv_root,
    off_leafs,
    off_mid,
    owner_leafs,
    offset_leafs,
    owner_mid,
    offset_mid,
):
    leaf_total = lax.axis_size("leaf")
    low_bits = leaf_total.bit_length() - 3
    mid_bits = low_bits + 1
    piece_rows = rhs_leafs.shape[0]
    panel_leafs = flat_panel(inv_leafs)
    panel_mid = flat_panel(inv_mid)
    panel_root = flat_panel(inv_root)
    solved_leafs = reduce_rows(panel_leafs, group_gather(rhs_leafs, low_bits))
    carried_leafs = route_update(
        off_leafs, owner_leafs, offset_leafs, solved_leafs, low_bits, 2 * piece_rows
    )
    input_mid = (rhs_mid.astype(jnp.float32) - carried_leafs[:piece_rows]).astype(jnp.bfloat16)
    solved_mid = reduce_rows(panel_mid, group_gather(input_mid, mid_bits))
    carried_mid = route_update(off_mid, owner_mid, offset_mid, solved_mid, mid_bits, piece_rows)
    input_root = (rhs_root.astype(jnp.float32) - carried_leafs[piece_rows:] - carried_mid).astype(
        jnp.bfloat16
    )
    gathered_root = lax.all_gather(input_root, "leaf", axis=0, tiled=True)
    solved_root = reduce_rows(panel_root, gathered_root)
    root_partial = transpose_block(panel_root, solved_root)
    solution_root = lax.psum_scatter(
        root_partial.astype(jnp.bfloat16), "leaf", scatter_dimension=0, tiled=True
    )
    chosen_mid = pick_rows(solution_root, owner_mid, offset_mid)
    back_partial = lax.dot_general(
        flat_panel(off_mid), chosen_mid, CONTRACT_ROWS, preferred_element_type=jnp.float32
    )
    back_mid = group_sum(back_partial, mid_bits)
    rest_mid = (solved_mid.astype(jnp.float32) - back_mid).astype(jnp.bfloat16)
    solution_mid = group_sum(transpose_block(panel_mid, rest_mid), mid_bits).astype(jnp.bfloat16)
    stacked = jnp.concatenate([solution_mid, solution_root], 0)
    chosen_leafs = pick_rows(stacked, owner_leafs, offset_leafs)
    back_partial_leafs = lax.dot_general(
        flat_panel(off_leafs), chosen_leafs, CONTRACT_ROWS, preferred_element_type=jnp.float32
    )
    back_leafs = group_sum(back_partial_leafs, low_bits)
    rest_leafs = (solved_leafs.astype(jnp.float32) - back_leafs).astype(jnp.bfloat16)
    solution_leafs = group_sum(transpose_block(panel_leafs, rest_leafs), low_bits).astype(
        jnp.bfloat16
    )
    return (solution_leafs, solution_mid, solution_root)


def solution(mesh):
    placed = (
        P(("leaf", "row", "col"), None),
        P(("leaf", "row", "col"), None),
        P(("leaf", "row", "col"), None),
        P("leaf", ("row", "col"), None),
        P("leaf", ("row", "col"), None),
        P("leaf", ("row", "col"), None),
        P("leaf", ("row", "col"), None),
        P("leaf", ("row", "col"), None),
        P("leaf", None),
        P("leaf"),
        P("leaf", None),
        P("leaf"),
    )
    return jax.shard_map(
        shards,
        mesh=mesh,
        in_specs=placed,
        out_specs=(
            P(("leaf", "row", "col"), None),
            P(("leaf", "row", "col"), None),
            P(("leaf", "row", "col"), None),
        ),
        check_vma=False,
    )
```

profile of v0, /device:TPU:1, one launch (start us, length us, event | category | flops | bytes accessed | tf_op | source)
XLA Modules:
  0.0 1190.0 jit_solution(14030300456103324859)
XLA Ops:
  7.2 8.9 collective-permute-start
  16.2 1.0 collective-permute-done
  17.2 1.9 collective-permute-start.1
  19.2 2.7 collective-permute-done.1
  21.9 1.3 fusion
  23.1 1.0 copy.65
  24.8 1.2 reduce-window.14
  26.4 2.4 scatter_custom_fusion
  28.9 209.6 %reduce-scatter.13.cloned.1.call-done = bf16[32,256]{1,0:T(8,128)(2,1)} async-done(((bf16[1024,256]{1,0:T(8,128)(2,1)}), bf16[32,256]{1,0:T(8,128)(2,1)}) %reduce-scatter.13.cloned.1.call-update) | async-done | bytes 16400 | tf_op jit(solution)/shard_map/reduce_scatter | solution.py:60
  238.4 7.7 collective-permute-start.2
  246.2 1.0 collective-permute-done.2
  248.0 3.1 collective-permute-start.3
  251.1 2.4 scatter_custom_fusion.1
  254.1 3.5 gather_fusion.2
  257.5 1.1 fusion.8
  258.7 6.4 all-to-all-start
  267.2 14.2 %all-to-all-done = bf16[32,32,256]{2,1,0:T(8,128)(2,1)S(1)} async-done(((bf16[32,32,256]{2,1,0:T(8,128)(2,1)}), bf16[32,32,256]{2,1,0:T(8,128)(2,1)S(1)}, u32[]{:S(2)}, u32[]{:S(2)}) %all-to-all-start) | async-done | bytes 524320 | tf_op jit(solution)/shard_map/all_to_all | solution.py:106
  282.2 4.3 collective-permute-start.4
  286.5 0.8 collective-permute-done.4
  287.3 2.3 collective-permute-start.5
  289.6 2.4 collective-permute-done.5
  292.0 4.0 collective-permute-start.6
  296.1 2.5 collective-permute-done.6
  299.0 1.0 copy.67
  300.0 1.2 reduce-window.16
  301.6 208.9 %reduce-scatter.15.cloned.1.call-done = bf16[32,256]{1,0:T(8,128)(2,1)} async-done(((bf16[1024,256]{1,0:T(8,128)(2,1)}), bf16[32,256]{1,0:T(8,128)(2,1)}) %reduce-scatter.15.cloned.1.call-update) | async-done | bytes 16400 | tf_op jit(solution)/shard_map/reduce_scatter | solution.py:60
  510.5 7.9 collective-permute-start.7
  518.4 2.4 scatter_custom_fusion.2
  520.9 3.1 collective-permute-start.8
  524.1 1.5 collective-permute-done.8
  525.6 4.1 collective-permute-start.9
  529.7 2.4 scatter_custom_fusion.3
  532.6 3.5 gather_fusion.3
  536.1 1.1 fusion.7
  537.2 6.4 all-to-all-start.1
  544.9 13.7 %all-to-all-done.1 = bf16[32,32,256]{2,1,0:T(8,128)(2,1)S(1)} async-done(((bf16[32,32,256]{2,1,0:T(8,128)(2,1)}), bf16[32,32,256]{2,1,0:T(8,128)(2,1)S(1)}, u32[]{:S(2)}, u32[]{:S(2)}) %all-to-all-start.1) | async-done | bytes 524320 | tf_op jit(solution)/shard_map/all_to_all | solution.py:106
  558.9 21.3 %all_gather.18 = bf16[512,256]{1,0:T(8,128)(2,1)S(1)} all-gather(bf16[32,256]{1,0:T(8,128)(2,1)S(1)} %fusion.4), channel_id=1, replica_groups=mesh['leaf'=16,'row'=8,'col'=4] {'leaf'}, dimensions={0}, use_global_device_ids=true | all-gather | bytes 278528 | tf_op jit(solution)/shard_map/all_gather | solution.py:148
  580.7 1.0 copy.69
  581.7 207.2 %reduce-scatter.17.cloned.1.call-done = bf16[32,256]{1,0:T(8,128)(2,1)} async-done(((bf16[1024,256]{1,0:T(8,128)(2,1)}), bf16[32,256]{1,0:T(8,128)(2,1)}) %reduce-scatter.17.cloned.1.call-update) | async-done | bytes 16400 | tf_op jit(solution)/shard_map/reduce_scatter | solution.py:60
  788.9 35.8 %all_gather.19 = bf16[1024,256]{1,0:T(8,128)(2,1)S(1)} all-gather(bf16[32,256]{1,0:T(8,128)(2,1)} %reduce-scatter.17.cloned.1.call-done), channel_id=1, replica_groups=mesh['leaf'=16,'row'=8,'col'=4] {'row','col'}, dimensions={0}, use_global_device_ids=true | all-gather | bytes 540672 | tf_op jit(solution)/shard_map/all_gather | solution.py:71
  825.2 0.8 copy.71
  826.1 72.3 %reduce-scatter.19.cloned.1.call-done = bf16[32,256]{1,0:T(8,128)(2,1)} async-done(((bf16[512,256]{1,0:T(8,128)(2,1)}), bf16[32,256]{1,0:T(8,128)(2,1)}) %reduce-scatter.19.cloned.1.call-update) | async-done | bytes 16400 | tf_op jit(solution)/shard_map/reduce_scatter | solution.py:151
  898.4 38.1 %all_gather.20 = bf16[1024,256]{1,0:T(8,128)(2,1)S(1)} all-gather(bf16[32,256]{1,0:T(8,128)(2,1)} %reduce-scatter.19.cloned.1.call-done), channel_id=1, replica_groups=mesh['leaf'=16,'row'=8,'col'=4] {'row','col'}, dimensions={0}, use_global_device_ids=true | all-gather | bytes 540672 | tf_op jit(solution)/shard_map/all_gather | solution.py:78
  936.5 1.9 gather_fusion
  938.8 4.9 collective-permute-start.10
  943.7 1.6 collective-permute-done.10
  945.4 5.2 collective-permute-start.11
  950.6 1.3 collective-permute-done.11
  951.9 17.0 %collective-permute-start.12 = (bf16[32,256]{1,0:T(8,128)(2,1)S(1)}, bf16[32,256]{1,0:T(8,128)(2,1)S(1)}, u32[]{:S(2)}, u32[]{:S(2)}) collective-permute-start(bf16[32,256]{1,0:T(8,128)(2,1)S(1)} %select_convert_fusion.9), channel_id=1, source_target_pairs={{0,32},{32,0},{64,96},{96,64},{128,160},{160,128},{192,224},{224,1... | collective-permute-start | bytes 49160 | tf_op jit(solution)/shard_map/ppermute | solution.py:20
  969.7 36.4 %all_gather.21 = bf16[1024,256]{1,0:T(8,128)(2,1)S(1)} all-gather(bf16[32,256]{1,0:T(8,128)(2,1)S(1)} %subtract_convert_fusion.1), channel_id=1, replica_groups=mesh['leaf'=16,'row'=8,'col'=4] {'row','col'}, dimensions={0}, use_global_device_ids=true | all-gather | bytes 540672 | tf_op jit(solution)/shard_map/all_gather | solution.py:71
  1006.5 1.9 collective-permute-start.13
  1008.4 4.1 collective-permute-done.13
  1012.6 1.9 collective-permute-start.14
  1014.5 3.0 collective-permute-done.14
  1017.6 16.0 %collective-permute-start.15 = (bf16[32,256]{1,0:T(8,128)(2,1)S(1)}, bf16[32,256]{1,0:T(8,128)(2,1)S(1)}, u32[]{:S(2)}, u32[]{:S(2)}) collective-permute-start(bf16[32,256]{1,0:T(8,128)(2,1)S(1)} %select_convert_fusion.8), channel_id=1, source_target_pairs={{0,32},{32,0},{64,96},{96,64},{128,160},{160,128},{192,224},{224,1... | collective-permute-start | bytes 49160 | tf_op jit(solution)/shard_map/ppermute | solution.py:20
  1035.2 73.1 %all-gather.2.cloned.1.call-done = bf16[2048,256]{1,0:T(8,128)(2,1)} async-done(((bf16[64,256]{1,0:T(8,128)(2,1)}), bf16[2048,256]{1,0:T(8,128)(2,1)}) %all-gather.2.cloned.1.call-update) | async-done | bytes 1048592 | tf_op jit(solution)/shard_map/all_gather | solution.py:78
  1108.3 2.9 gather_fusion.1
  1111.6 3.1 collective-permute-start.16
  1114.7 1.5 collective-permute-done.16
  1116.3 8.2 collective-permute-start.17
  1125.3 36.6 %all_gather.23 = bf16[1024,256]{1,0:T(8,128)(2,1)S(1)} all-gather(bf16[32,256]{1,0:T(8,128)(2,1)S(1)} %subtract_convert_fusion), channel_id=1, replica_groups=mesh['leaf'=16,'row'=8,'col'=4] {'row','col'}, dimensions={0}, use_global_device_ids=true | all-gather | bytes 540672 | tf_op jit(solution)/shard_map/all_gather | solution.py:71
  1162.2 3.1 collective-permute-start.18
  1165.3 1.8 collective-permute-done.18
  1167.2 14.8 %collective-permute-start.19 = (bf16[32,256]{1,0:T(8,128)(2,1)S(1)}, bf16[32,256]{1,0:T(8,128)(2,1)S(1)}, u32[]{:S(2)}, u32[]{:S(2)}) collective-permute-start(bf16[32,256]{1,0:T(8,128)(2,1)S(1)} %select_convert_fusion.6), channel_id=1, source_target_pairs={{0,32},{32,0},{64,96},{96,64},{128,160},{160,128},{192,224},{224,1... | collective-permute-start | bytes 49160 | tf_op jit(solution)/shard_map/ppermute | solution.py:20
  (120 shorter events, 15.2 us)
Async XLA Ops:
  7.2 573.0 %copy-start = (bf16[1024,1,512]{2,0,1:T(8,128)(2,1)S(1)}, bf16[1024,1,512]{2,0,1:T(8,128)(2,1)}, u32[]{:S(2)}) copy-start(bf16[1024,1,512]{2,0,1:T(8,128)(2,1)} %param.19) | copy-start | bytes 3145732
  7.2 10.0 copy-start.13
  7.2 231.2 %reduce-scatter.13.cloned.1.call-start = ((), (), s32[]{:S(2)}) async-start(), calls=%async_computation.7 | async-start | bytes 540672 | tf_op jit(solution)/shard_map/reduce_scatter | solution.py:60
  7.2 10.0 collective-permute-start
  17.2 4.7 collective-permute-start.1
  24.1 0.7 copy-start.11
  26.0 227.6 %copy-start.4 = (bf16[512,1,128]{2,0,1:T(8,128)(2,1)S(1)}, bf16[512,1,128]{2,0,1:T(8,128)(2,1)}, u32[]{:S(2)}) copy-start(bf16[512,1,128]{2,0,1:T(8,128)(2,1)} %param.20) | copy-start | bytes 393220
  238.4 8.8 collective-permute-start.2
  248.0 5.6 collective-permute-start.3
  258.7 22.7 %all-to-all-start = ((bf16[32,32,256]{2,1,0:T(8,128)(2,1)}), bf16[32,32,256]{2,1,0:T(8,128)(2,1)S(1)}, u32[]{:S(2)}, u32[]{:S(2)}) async-start(bf16[32,32,256]{2,1,0:T(8,128)(2,1)} %bitcast.10), calls=%async_computation | async-start | bytes 1048576 | tf_op jit(solution)/shard_map/all_to_all | solution.py:106
  265.1 245.4 %reduce-scatter.15.cloned.1.call-start = ((), (), s32[]{:S(2)}) async-start(), calls=%async_computation.8 | async-start | bytes 540672 | tf_op jit(solution)/shard_map/reduce_scatter | solution.py:60
  265.2 0.7 copy-start.10
  265.8 0.7 copy-start.16
  267.2 31.5 %copy-start.1 = (bf16[1024,1,256]{2,0,1:T(8,128)(2,1)S(1)}, bf16[1024,1,256]{2,0,1:T(8,128)(2,1)}, u32[]{:S(2)}) copy-start(bf16[1024,1,256]{2,0,1:T(8,128)(2,1)} %param.18) | copy-start | bytes 1572868
  281.5 0.7 copy-start.14
  282.2 5.1 collective-permute-start.4
  287.3 4.7 collective-permute-start.5
  292.0 6.6 collective-permute-start.6
  300.0 232.1 %copy-start.3 = (bf16[512,1,256]{2,0,1:T(8,128)(2,1)S(1)}, bf16[512,1,256]{2,0,1:T(8,128)(2,1)}, u32[]{:S(2)}) copy-start(bf16[512,1,256]{2,0,1:T(8,128)(2,1)} %param.21) | copy-start | bytes 786436
  510.5 10.4 copy-start.8
  510.5 10.3 collective-permute-start.7
  520.9 4.7 collective-permute-start.8
  525.6 6.6 collective-permute-start.9
  537.2 21.4 %all-to-all-start.1 = ((bf16[32,32,256]{2,1,0:T(8,128)(2,1)}), bf16[32,32,256]{2,1,0:T(8,128)(2,1)S(1)}, u32[]{:S(2)}, u32[]{:S(2)}) async-start(bf16[32,32,256]{2,1,0:T(8,128)(2,1)} %bitcast.21), calls=%async_computation.1 | async-start | bytes 1048576 | tf_op jit(solution)/shard_map/all_to_all | solution.py:106
  543.6 0.7 copy-start.15
  543.6 245.3 %reduce-scatter.17.cloned.1.call-start = ((), (), s32[]{:S(2)}) async-start(), calls=%async_computation.9 | async-start | bytes 540672 | tf_op jit(solution)/shard_map/reduce_scatter | solution.py:60
  544.9 13.8 %copy-start.12 = (bf16[32,256]{1,0:T(8,128)(2,1)S(1)}, bf16[32,256]{1,0:T(8,128)(2,1)}, u32[]{:S(2)}) copy-start(bf16[32,256]{1,0:T(8,128)(2,1)} %param.16) | copy-start | bytes 49156
  581.7 316.7 %reduce-scatter.19.cloned.1.call-start = ((), (), s32[]{:S(2)}) async-start(), calls=%async_computation.10 | async-start | bytes 278528 | tf_op jit(solution)/shard_map/reduce_scatter | solution.py:151
  826.0 282.3 %all-gather.2.cloned.1.call-start = ((), (), s32[]{:S(2)}) async-start(), calls=%async_computation.6 | async-start | bytes 1081344 | tf_op jit(solution)/shard_map/all_gather | solution.py:78
  938.8 6.5 collective-permute-start.10
  945.4 6.5 collective-permute-start.11
  951.9 17.8 %collective-permute-start.12 = (bf16[32,256]{1,0:T(8,128)(2,1)S(1)}, bf16[32,256]{1,0:T(8,128)(2,1)S(1)}, u32[]{:S(2)}, u32[]{:S(2)}) collective-permute-start(bf16[32,256]{1,0:T(8,128)(2,1)S(1)} %select_convert_fusion.9), channel_id=1, source_target_pairs={{0,32},{32,0},{64,96},{96,64},{128,160},{160,128},{192,224},{224,1... | collective-permute-start | bytes 49160 | tf_op jit(solution)/shard_map/ppermute | solution.py:20
  1006.5 6.1 collective-permute-start.13
  1012.6 5.0 collective-permute-start.14
  1017.6 16.9 %copy-start.7 = (bf16[32,256]{1,0:T(8,128)(2,1)S(1)}, bf16[32,256]{1,0:T(8,128)(2,1)}, u32[]{:S(2)}) copy-start(bf16[32,256]{1,0:T(8,128)(2,1)} %reduce-scatter.19.cloned.1.call-done) | copy-start | bytes 49156
  1017.6 16.9 %collective-permute-start.15 = (bf16[32,256]{1,0:T(8,128)(2,1)S(1)}, bf16[32,256]{1,0:T(8,128)(2,1)S(1)}, u32[]{:S(2)}, u32[]{:S(2)}) collective-permute-start(bf16[32,256]{1,0:T(8,128)(2,1)S(1)} %select_convert_fusion.8), channel_id=1, source_target_pairs={{0,32},{32,0},{64,96},{96,64},{128,160},{160,128},{192,224},{224,1... | collective-permute-start | bytes 49160 | tf_op jit(solution)/shard_map/ppermute | solution.py:20
  1034.5 0.6 copy-start.9
  1035.2 76.1 %copy-start.5 = (bf16[512,1,128]{2,0,1:T(8,128)(2,1)S(1)}, bf16[512,1,128]{2,0,1:T(8,128)(2,1)}, u32[]{:S(2)}) copy-start(bf16[512,1,128]{2,0,1:T(8,128)(2,1)} %param.20) | copy-start | bytes 393220
  1111.6 4.7 collective-permute-start.16
  1116.3 9.0 copy-start.6
  1116.3 9.0 collective-permute-start.17
  1125.3 36.6 %copy-start.2 = (bf16[1024,1,128]{2,0,1:T(8,128)(2,1)S(1)}, bf16[1024,1,128]{2,0,1:T(8,128)(2,1)}, u32[]{:S(2)}) copy-start(bf16[1024,1,128]{2,0,1:T(8,128)(2,1)} %param.17) | copy-start | bytes 786436
  1162.2 5.0 collective-permute-start.18
  1167.2 15.6 %collective-permute-start.19 = (bf16[32,256]{1,0:T(8,128)(2,1)S(1)}, bf16[32,256]{1,0:T(8,128)(2,1)S(1)}, u32[]{:S(2)}, u32[]{:S(2)}) collective-permute-start(bf16[32,256]{1,0:T(8,128)(2,1)S(1)} %select_convert_fusion.6), channel_id=1, source_target_pairs={{0,32},{32,0},{64,96},{96,64},{128,160},{160,128},{192,224},{224,1... | collective-permute-start | bytes 49160 | tf_op jit(solution)/shard_map/ppermute | solution.py:20
Sparse Core Ops, SparseCore 0:
  24.3 214.0 reduce-scatter.12
  300.1 210.3 reduce-scatter.14
  581.8 207.0 reduce-scatter.16
  826.1 72.1 reduce-scatter.18
  1035.3 73.0 all-gather.1
where the time goes:
time: 1190 us
  waiting for transfers between devices  828 us (70%)
  blocking collectives  168 us (14%)
  starting transfers between devices  136 us (11%)
  local copies, waits for them, and re-layouts  29.4 us (2%)
  between operations  14.6 us (1%)
    reduce_scatter x3, waiting for transfers between devices, reduce_rows(): lax.psum_scatter(jnp.dot(panels, gathered, preferred_element_type=jnp.flo...  626 us
    ppermute x20, starting transfers between devices, partner_2(): return lax.ppermute(block, axis, route)  124 us
    all_gather x3, blocking collectives, transpose_block(): lax.all_gather(column_rows, ('row', 'col'), axis=0, tiled=True)  109 us
    all_gather x1, waiting for transfers between devices, pick_rows(): gathered = lax.all_gather(ancestor, ('row', 'col'), axis=0, tiled=True)  73.1 us
    reduce_scatter x1, waiting for transfers between devices, shards(): lax.psum_scatter(root_partial.astype(jnp.bfloat16), 'leaf', scatter_dimen...  72.3 us
    all_gather x1, blocking collectives, pick_rows(): gathered = lax.all_gather(ancestor, ('row', 'col'), axis=0, tiled=True)  38.1 us
    ppermute x20, waiting for transfers between devices, partner_2(): return lax.ppermute(block, axis, route)  28.7 us
    all_to_all x2, waiting for transfers between devices, route_update(): lax.all_to_all(outgoing.astype(jnp.bfloat16), ('row', 'col'), split_axis=...  27.9 us
  transfers between devices with their start and end apart: 27, of which 24 were waited for; matrix products, arithmetic and copies ran while one was open for 1% of the time, Pallas kernels for 0%

commit v1 on v0

v1 whole, which is shorter than its diff:
```python
import functools

import jax
import jax.numpy as jnp
from jax import lax
from jax.experimental import pallas as pl
from jax.experimental.pallas import tpu as pltpu
from jax.sharding import PartitionSpec as P

MESH = pl.DeviceIdType.MESH
BF = jnp.bfloat16
F32 = jnp.float32
ROWS = 32
NRHS = 256
PARTS = 1
CHUNK = 1


def z_order(nz):
    order = []
    for near in range(nz // 2, 0, -1):
        order.append(near)
        if nz - near != near:
            order.append(nz - near)
    return order + [0]


def dot(a, b):
    return jnp.dot(a, b, preferred_element_type=F32)


def dot_nt(a, b):
    return lax.dot_general(a, b, (((1,), (1,)), ((), ())), preferred_element_type=F32)


def one_hot(condition):
    return jnp.where(condition, 1.0, 0.0).astype(BF)


def kernel(sizes, *refs):
    names, groups, nz, nx = sizes
    r = dict(zip(names, refs, strict=True))
    width = NRHS // PARTS
    leaf, z, x = lax.axis_index("leaf"), lax.axis_index("row"), lax.axis_index("col")
    order = z_order(nz)
    rows = nz * nx * ROWS
    nleaf = groups[4]

    loads = {}
    for number, name in enumerate(("rl", "i1", "w1", "o1", "f1", "rm", "i2", "rr", "w2", "o2", "f2", "i3")):
        loads[name] = pltpu.make_async_copy(r["in_" + name], r["v_" + name], r["load"].at[number])
        loads[name].start()

    barrier = pltpu.get_barrier_semaphore()
    for d in range(1, nleaf):
        pl.semaphore_signal(barrier, inc=1, device_id=(lax.rem(leaf + d, nleaf), z, x), device_id_type=MESH)
    for d in range(1, nz):
        pl.semaphore_signal(barrier, inc=1, device_id=(leaf, lax.rem(z + d, nz), x), device_id_type=MESH)
    for d in range(1, nx):
        pl.semaphore_signal(barrier, inc=1, device_id=(leaf, z, lax.rem(x + d, nx)), device_id_type=MESH)

    def send(source, target, send_sem, recv_sem, where):
        pltpu.make_async_remote_copy(
            src_ref=source, dst_ref=target, send_sem=send_sem, recv_sem=recv_sem, device_id=where, device_id_type=MESH
        ).start()

    def wait(ref, sem):
        pltpu.make_async_copy(ref, ref, sem).wait()

    def member(k):
        return lax.rem(leaf, groups[k])

    def columns(h):
        return slice(h * width, (h + 1) * width)

    def gather_start(k, h, block):
        count, me, buf = groups[k], member(k), r[f"gat{k}"]
        buf[h, me] = block
        for d in range(1, count):
            there = leaf - me + lax.rem(me + d, count)
            send(buf.at[h, me], buf.at[h, me], r["gs"].at[k, h], r["gr"].at[k, h], (there, z, x))

    def multiply_start(k, h, panel):
        count, buf, prod, land = groups[k], r[f"gat{k}"], r[f"prod{k}"], r[f"rx{k}"]
        wait(buf.at[h, 0 : count - 1], r["gr"].at[k, h])
        vector = buf[h].reshape(count * ROWS, width)
        for pos, j in enumerate(order):
            there = lax.rem(z + j, nz)
            first = pl.multiple_of(there * (nx * ROWS), nx * ROWS)
            block = dot(panel[pl.ds(first, nx * ROWS), :], vector).astype(BF)
            for c in range(nx):
                prod[h, c, pos] = block[c * ROWS : (c + 1) * ROWS]
            if (pos + 1) % CHUNK == 0:
                cut = pl.ds(pos + 1 - CHUNK, CHUNK)
                for d in range(1, nx):
                    c = lax.rem(x + d, nx)
                    send(prod.at[h, c, cut], land.at[h, d - 1, cut], r["xs"].at[k, h], r["xr"].at[k, h, pos // CHUNK], (leaf, z, c))

    def reduce_x(k, h):
        prod, land, sums, final = r[f"prod{k}"], r[f"rx{k}"], r[f"sum{k}"], r[f"rz{k}"]
        own = None
        for pos, j in enumerate(order):
            if pos % CHUNK == 0:
                cut = pl.ds(pos, CHUNK)
                wait(land.at[h, :, cut], r["xr"].at[k, h, pos // CHUNK])
            total = prod[h, x, pos].astype(F32)
            for d in range(1, nx):
                total += land[h, d - 1, pos].astype(F32)
            if j == 0:
                own = total
            else:
                sums[h, pos] = total.astype(BF)
                send(sums.at[h, pos], final.at[h, j - 1], r["zs"].at[k, h], r["zr"].at[k, h], (leaf, lax.rem(z + j, nz), x))
        return own

    def reduce_z(k, h, own):
        final = r[f"rz{k}"]
        wait(final.at[h], r["zr"].at[k, h])
        total = own
        for j in range(1, nz):
            total += final[h, j - 1].astype(F32)
        return total

    def forward_sent(k):
        for h in range(PARTS):
            wait(r[f"gat{k}"].at[h, 0 : groups[k] - 1], r["gs"].at[k, h])
            wait(r[f"rx{k}"].at[h], r["xs"].at[k, h])
            wait(r[f"rz{k}"].at[h], r["zs"].at[k, h])

    def spread_x(k, h, row):
        buf = r[f"all{k}"]
        for d in range(1, nx):
            send(buf.at[h, row, x], buf.at[h, row, x], r["bxs"].at[k, h], r["bxr"].at[k, h], (leaf, z, lax.rem(x + d, nx)))

    def spread_start(k, h, block):
        buf = r[f"all{k}"]
        buf[h, z, x] = block
        for j in order[:-1]:
            send(buf.at[h, z, x], buf.at[h, z, x], r["bzs"].at[k, h], r["bzr"].at[k, h, j - 1], (leaf, lax.rem(z + j, nz), x))
        spread_x(k, h, z)

    def spread_on(k, h):
        buf = r[f"all{k}"]
        for j in reversed(order[:-1]):
            row = lax.rem(z + nz - j, nz)
            wait(buf.at[h, row, x], r["bzr"].at[k, h, j - 1])
            spread_x(k, h, row)

    def transposed_start(k, h, panel):
        buf, part, exact, land, count, me = r[f"all{k}"], r[f"part{k}"], r[f"exact{k}"], r[f"lr{k}"], groups[k], member(k)
        wait(buf.at[h, :, 0 : nx - 1], r["bxr"].at[k, h])
        result = dot(panel[...], buf[h].reshape(rows, width)).reshape(count, ROWS, width)
        exact[h] = result
        part[h] = result.astype(BF)
        for d in range(1, count):
            m = lax.rem(me + d, count)
            send(part.at[h, m], land.at[h, d - 1], r["ls"].at[k, h], r["lr"].at[k, h], (leaf - me + m, z, x))

    def transposed_end(k, h):
        exact, land = r[f"exact{k}"], r[f"lr{k}"]
        wait(land.at[h], r["lr"].at[k, h])
        total = exact[h, member(k)]
        for d in range(1, groups[k]):
            total += land[h, d - 1].astype(F32)
        return total

    def backward_sent(k):
        for h in range(PARTS):
            wait(r[f"all{k}"].at[h, 0 : nz - 1, 0], r["bzs"].at[k, h])
            wait(r[f"all{k}"].at[h, :, 0 : nx - 1], r["bxs"].at[k, h])
            wait(r[f"lr{k}"].at[h], r["ls"].at[k, h])

    def slots(name):
        ids = r["v_w" + name][...]
        places = ids.shape[1]
        blocks = nz * nx
        mine = jnp.broadcast_to(ids, (blocks, places)) == lax.broadcasted_iota(jnp.int32, (blocks, places), 0)
        before = lax.broadcasted_iota(jnp.int32, (places, places), 0) < lax.broadcasted_iota(jnp.int32, (places, places), 1)
        rank = jnp.where(mine, dot(one_hot(mine), one_hot(before)), -1.0)
        slot = lax.broadcasted_iota(jnp.int32, (ROWS, places), 0).astype(F32)
        for b in range(blocks):
            r["perm"][b] = one_hot(jnp.broadcast_to(rank[b : b + 1, :], (ROWS, places)) == slot)
        r["p" + name][...] = dot(r["perm"][...].reshape(blocks * ROWS, places), r["v_o" + name][...]).astype(BF)
        own = r["perm"][z * nx + x]
        targets = r["lay" + name].shape[0]
        offset = jnp.broadcast_to(r["v_f" + name][...], (targets, places))
        wanted = one_hot(offset == lax.broadcasted_iota(jnp.int32, (targets, places), 0))
        r["lay" + name][...] = dot_nt(wanted, own).astype(BF)
        r["sel" + name][...] = dot_nt(own, wanted).astype(BF)

    def to_targets(name, total):
        high = total.astype(BF)
        low = (total - high.astype(F32)).astype(BF)
        return dot(r["lay" + name][...], high) + dot(r["lay" + name][...], low)

    def transpose(name, panel):
        r["t_" + name][...] = panel[...].T

    halves = range(PARTS)

    def forward(k, blocks, panel, after_gather=None, after_x=None):
        for h in halves:
            gather_start(k, h, blocks[h])
        if after_gather is not None:
            after_gather()
        for h in halves:
            multiply_start(k, h, panel)
        if after_x is not None:
            after_x()
        own = [reduce_x(k, h) for h in halves]
        return [reduce_z(k, h, own[h]) for h in halves]

    def backward(k, blocks, panel, before=None):
        for h in halves:
            spread_start(k, h, blocks[h])
        for h in halves:
            spread_on(k, h)
        if before is not None:
            before()
        for h in halves:
            transposed_start(k, h, panel)
        return [transposed_end(k, h) for h in halves]

    def load(*wanted):
        for name in wanted:
            loads[name].wait()

    load("rl")
    pl.semaphore_wait(barrier, nleaf + nz + nx - 3)

    def prepare_leafs():
        load("w1", "o1", "f1")
        slots("1")

    def prepare_mid():
        load("w2", "o2", "f2")
        slots("2")

    total = forward(0, [r["v_rl"][:, columns(h)] for h in halves], r["v_i1"], lambda: load("i1"), prepare_leafs)
    solved_leafs = [t.astype(BF) for t in total]
    total = forward(1, solved_leafs, r["p1"], None, prepare_mid)
    carried = [to_targets("1", t) for t in total]
    load("rm")
    blocks = [(r["v_rm"][:, columns(h)].astype(F32) - carried[h][:ROWS]).astype(BF) for h in halves]
    total = forward(2, blocks, r["v_i2"], lambda: load("i2"), lambda: transpose("p1", r["p1"]))
    solved_mid = [t.astype(BF) for t in total]
    total = forward(3, solved_mid, r["p2"], None, lambda: transpose("p2", r["p2"]))
    load("rr")
    blocks = [
        (r["v_rr"][:, columns(h)].astype(F32) - carried[h][ROWS:] - to_targets("2", total[h])).astype(BF) for h in halves
    ]
    load("i3")
    total = forward(4, blocks, r["v_i3"], lambda: transpose("i3", r["v_i3"]), lambda: transpose("i2", r["v_i2"]))

    total = backward(4, [t.astype(BF) for t in total], r["t_i3"], lambda: transpose("i1", r["v_i1"]))
    solution_root = [t.astype(BF) for t in total]
    for h in halves:
        r["out_r"][:, columns(h)] = solution_root[h]
    total = backward(3, [dot(r["sel2"][...], solution_root[h]).astype(BF) for h in halves], r["t_p2"])
    rest = [(solved_mid[h].astype(F32) - total[h]).astype(BF) for h in halves]
    total = backward(2, rest, r["t_i2"])
    solution_mid = [t.astype(BF) for t in total]
    for h in halves:
        r["out_m"][:, columns(h)] = solution_mid[h]
    stacked = [jnp.concatenate([solution_mid[h], solution_root[h]], 0) for h in halves]
    total = backward(1, [dot(r["sel1"][...], stacked[h]).astype(BF) for h in halves], r["t_p1"])
    rest = [(solved_leafs[h].astype(F32) - total[h]).astype(BF) for h in halves]
    total = backward(0, rest, r["t_i1"])
    for h in halves:
        r["out_l"][:, columns(h)] = total[h].astype(BF)

    for k in range(5):
        forward_sent(k)
        backward_sent(k)


def shards(
    mesh_shape,
    rhs_leafs,
    rhs_mid,
    rhs_root,
    inv_leafs,
    inv_mid,
    inv_root,
    off_leafs,
    off_mid,
    owner_leafs,
    offset_leafs,
    owner_mid,
    offset_mid,
):
    nleaf, nz, nx = mesh_shape
    groups = (nleaf // 4, nleaf // 4, nleaf // 2, nleaf // 2, nleaf)
    width = NRHS // PARTS
    rows = nz * nx * ROWS

    def flat(panel):
        return panel.reshape(panel.shape[0], panel.shape[2])

    operands = {
        "rl": rhs_leafs,
        "rm": rhs_mid,
        "rr": rhs_root,
        "i1": flat(inv_leafs),
        "i2": flat(inv_mid),
        "i3": flat(inv_root),
        "o1": flat(off_leafs),
        "o2": flat(off_mid),
        "w1": owner_leafs.reshape(1, -1),
        "f1": offset_leafs.reshape(1, -1),
        "w2": owner_mid.reshape(1, -1),
        "f2": offset_mid.reshape(1, -1),
    }
    places = off_leafs.shape[0]
    names = ["in_" + name for name in operands] + ["out_l", "out_m", "out_r"]
    scratch = []

    def keep(name, shape, dtype=BF):
        names.append(name)
        scratch.append(pltpu.VMEM(shape, dtype))

    def semaphores(name, shape):
        names.append(name)
        scratch.append(pltpu.SemaphoreType.DMA(shape))

    for name, value in operands.items():
        keep("v_" + name, value.shape, value.dtype)
    semaphores("load", (len(operands),))
    keep("perm", (nz * nx, ROWS, places))
    for name, panel, targets in (("1", operands["o1"], 2 * ROWS), ("2", operands["o2"], ROWS)):
        keep("p" + name, (rows, panel.shape[1]))
        keep("t_p" + name, (panel.shape[1], rows))
        keep("lay" + name, (targets, ROWS))
        keep("sel" + name, (ROWS, targets))
    for name in ("i1", "i2", "i3"):
        keep("t_" + name, operands[name].shape[::-1])
    for k, count in enumerate(groups):
        keep(f"gat{k}", (PARTS, count, ROWS, width))
        keep(f"prod{k}", (PARTS, nx, nz, ROWS, width))
        keep(f"rx{k}", (PARTS, nx - 1, nz, ROWS, width))
        keep(f"sum{k}", (PARTS, nz, ROWS, width))
        keep(f"rz{k}", (PARTS, nz - 1, ROWS, width))
        keep(f"all{k}", (PARTS, nz, nx, ROWS, width))
        keep(f"part{k}", (PARTS, count, ROWS, width))
        keep(f"exact{k}", (PARTS, count, ROWS, width), F32)
        keep(f"lr{k}", (PARTS, count - 1, ROWS, width))
    for name in ("gs", "gr", "xs", "zs", "zr", "bzs", "bxs", "bxr", "ls", "lr"):
        semaphores(name, (5, PARTS))
    semaphores("xr", (5, PARTS, nz // CHUNK))
    semaphores("bzr", (5, PARTS, nz - 1))

    block = jax.ShapeDtypeStruct(rhs_leafs.shape, rhs_leafs.dtype)
    return pl.pallas_call(
        functools.partial(kernel, (tuple(names), groups, nz, nx)),
        out_shape=(block, block, block),
        in_specs=[pl.BlockSpec(memory_space=pl.ANY)] * len(operands),
        out_specs=[pl.BlockSpec(memory_space=pltpu.VMEM)] * 3,
        scratch_shapes=scratch,
        compiler_params=pltpu.CompilerParams(collective_id=0, has_side_effects=True, vmem_limit_bytes=50 * 2**20),
        cost_estimate=pl.CostEstimate(flops=1_200_000_000, bytes_accessed=2_400_000, transcendentals=0),
        name="triangular_solve",
    )(*operands.values())


def solution(mesh):
    vector = P(("leaf", "row", "col"), None)
    panel = P("leaf", ("row", "col"), None)
    return jax.shard_map(
        functools.partial(shards, (mesh.shape["leaf"], mesh.shape["row"], mesh.shape["col"])),
        mesh=mesh,
        in_specs=(vector,) * 3 + (panel,) * 5 + (P("leaf", None), P("leaf")) * 2,
        out_specs=(vector,) * 3,
        check_vma=False,
    )
```

time: 1190 us -> 188 us (0.16)
  waiting for transfers between devices: 828 us -> 0 us
  Pallas kernels: 0 us -> 175 us
  blocking collectives: 168 us -> 0 us
  starting transfers between devices: 136 us -> 0 us
  local copies, waits for them, and re-layouts: 29.4 us -> 11.8 us
  between operations: 14.6 us -> 0.66 us
    reduce_scatter x4 -> x0, waiting for transfers between devices: 698 us -> none  [the longest x3 626 us: reduce_rows(): lax.psum_scatter(jnp.dot(panels, gathered, preferred_element_type=jnp.flo...]
    pallas_call x0 -> x1, Pallas kernels: none -> 175 us  [shards(): pl.pallas_call(functools.partial(kernel, (tuple(names), groups, nz, nx)),...]
    all_gather x5 -> x0, blocking collectives: 168 us -> none  [the longest x3 109 us: transpose_block(): lax.all_gather(column_rows, ('row', 'col'), axis=0, tiled=True)]
    ppermute x20 -> x0, starting transfers between devices: 124 us -> none  [partner_2(): return lax.ppermute(block, axis, route)]
    all_gather x1 -> x0, waiting for transfers between devices: 73.1 us -> none  [pick_rows(): gathered = lax.all_gather(ancestor, ('row', 'col'), axis=0, tiled=True)]
    ppermute x20 -> x0, waiting for transfers between devices: 28.7 us -> none  [partner_2(): return lax.ppermute(block, axis, route)]
    all_to_all x2 -> x0, waiting for transfers between devices: 27.9 us -> none  [route_update(): lax.all_to_all(outgoing.astype(jnp.bfloat16), ('row', 'col'), split_axis=...]
    all_to_all x2 -> x0, starting transfers between devices: 12.8 us -> none  [route_update(): lax.all_to_all(outgoing.astype(jnp.bfloat16), ('row', 'col'), split_axis=...]
  transfers between devices with their start and end apart: 27 -> 0, of which waited for: 24 -> 0; matrix products, arithmetic and copies ran while one was open for 1% -> 0% of each run, Pallas kernels for 0% -> 0%
where the time goes in v1:
time: 188 us
  Pallas kernels  175 us (93%)
  local copies, waits for them, and re-layouts  11.8 us (6%)
    pallas_call x1, Pallas kernels, shards(): pl.pallas_call(functools.partial(kernel, (tuple(names), groups, nz, nx)),...  175 us
    unnamed x27, local copies, waits for them, and re-layouts  11.8 us

profile of v1, /device:TPU:1, one launch (start us, length us, event | category | flops | bytes accessed | tf_op | source)
XLA Modules:
  0.0 187.8 jit_solution(3545436960789488041)
XLA Ops:
  0.6 0.0 copy-start.5
  0.6 0.7 copy-done.5
  1.4 0.0 copy-start
  1.4 1.2 copy-done
  2.6 0.0 copy-start.1
  2.6 1.0 copy-done.1
  3.6 0.0 copy-start.2
  3.6 0.9 copy-done.2
  4.6 0.0 copy-start.3
  4.6 0.9 copy-done.3
  5.5 0.0 copy-start.4
  5.5 0.9 copy-done.4
  6.4 0.0 copy-start.6
  6.4 0.7 copy-done.6
  7.1 0.0 copy-start.7
  7.1 0.7 copy-done.7
  7.9 0.0 copy-start.8
  7.9 0.7 copy-done.8
  8.5 0.0 copy-start.9
  8.5 0.7 copy-done.9
  9.2 0.0 copy-start.10
  9.2 0.7 copy-done.10
  9.9 0.0 copy-start.11
  9.9 0.7 copy-done.11
  10.6 175.4 %triangular_solve.1 = (bf16[32,256]{1,0:T(8,128)(2,1)S(1)}, bf16[32,256]{1,0:T(8,128)(2,1)S(1)}, bf16[32,256]{1,0:T(8,128)(2,1)S(1)}) custom-call(bf16[32,256]{1,0:T(8,128)(2,1)S(1)} %copy-done.5, bf16[32,256]{1,0:T(8,128)(2,1)S(1)} %copy-done.6, bf16[32,256]{1,0:T(8,128)(2,1)S(1)} %copy-done.7, bf16[1024,128]{1,0:T(8,128)(2,1)S(1)} %bitcast.11, ...), custom_call_target="tpu_custom_call" | custom-call | flops 1200000000 | bytes 2400000 | tf_op jit(solution)/shard_map/triangular_solve/pallas_call | solution.py:353
  186.0 0.6 copy.18
  186.6 0.6 copy.19
  187.2 0.6 copy.20
Async XLA Ops:
  0.6 0.7 copy-start.5
  1.4 1.2 copy-start
  2.6 1.0 copy-start.1
  3.6 0.9 copy-start.2
  4.6 0.9 copy-start.3
  5.5 0.9 copy-start.4
  6.4 0.7 copy-start.6
  7.1 0.7 copy-start.7
  7.9 0.7 copy-start.8
  8.5 0.7 copy-start.9
  9.2 0.7 copy-start.10
  9.9 0.7 copy-start.11

commit v2 on v1

--- a/solution.py
+++ b/solution.py
@@ -12,8 +12,9 @@
 F32 = jnp.float32
 ROWS = 32
 NRHS = 256
-PARTS = 1
+PARTS = 2
 CHUNK = 1
+LEAD = 1
 
 
 def z_order(nz):
@@ -45,6 +46,9 @@
     order = z_order(nz)
     rows = nz * nx * ROWS
     nleaf = groups[4]
+    y_order = z_order(nleaf // 2)
+    x_order = z_order(nx)[:-1]
+    sibling = leaf + 1 - 2 * lax.rem(leaf, 2)
 
     loads = {}
     for number, name in enumerate(("rl", "i1", "w1", "o1", "f1", "rm", "i2", "rr", "w2", "o2", "f2", "i3")):
@@ -73,16 +77,35 @@
     def columns(h):
         return slice(h * width, (h + 1) * width)
 
+    def is_wide(k):
+        return groups[k] == nleaf
+
     def gather_start(k, h, block):
         count, me, buf = groups[k], member(k), r[f"gat{k}"]
         buf[h, me] = block
+        if is_wide(k):
+            own = buf.at[h, me]
+            for d in y_order[:-1]:
+                send(own, own, r["gs"].at[k, h], r["gyr"].at[h, d - 1], (lax.rem(leaf + 2 * d, nleaf), z, x))
+            send(own, own, r["gs"].at[k, h], r["gr"].at[k, h], (sibling, z, x))
+            return
         for d in range(1, count):
             there = leaf - me + lax.rem(me + d, count)
             send(buf.at[h, me], buf.at[h, me], r["gs"].at[k, h], r["gr"].at[k, h], (there, z, x))
 
+    def gather_wait(k, h):
+        count, buf = groups[k], r[f"gat{k}"]
+        if is_wide(k):
+            for d in reversed(y_order[:-1]):
+                m = lax.rem(leaf + nleaf - 2 * d, nleaf)
+                wait(buf.at[h, m], r["gyr"].at[h, d - 1])
+                send(buf.at[h, m], buf.at[h, m], r["gs"].at[k, h], r["gr"].at[k, h], (sibling, z, x))
+            wait(buf.at[h, 0 : nleaf // 2], r["gr"].at[k, h])
+        else:
+            wait(buf.at[h, 0 : count - 1], r["gr"].at[k, h])
+
     def multiply_start(k, h, panel):
         count, buf, prod, land = groups[k], r[f"gat{k}"], r[f"prod{k}"], r[f"rx{k}"]
-        wait(buf.at[h, 0 : count - 1], r["gr"].at[k, h])
         vector = buf[h].reshape(count * ROWS, width)
         for pos, j in enumerate(order):
             there = lax.rem(z + j, nz)
@@ -92,7 +115,7 @@
                 prod[h, c, pos] = block[c * ROWS : (c + 1) * ROWS]
             if (pos + 1) % CHUNK == 0:
                 cut = pl.ds(pos + 1 - CHUNK, CHUNK)
-                for d in range(1, nx):
+                for d in x_order:
                     c = lax.rem(x + d, nx)
                     send(prod.at[h, c, cut], land.at[h, d - 1, cut], r["xs"].at[k, h], r["xr"].at[k, h, pos // CHUNK], (leaf, z, c))
 
@@ -121,15 +144,26 @@
             total += final[h, j - 1].astype(F32)
         return total
 
-    def forward_sent(k):
-        for h in range(PARTS):
-            wait(r[f"gat{k}"].at[h, 0 : groups[k] - 1], r["gs"].at[k, h])
-            wait(r[f"rx{k}"].at[h], r["xs"].at[k, h])
-            wait(r[f"rz{k}"].at[h], r["zs"].at[k, h])
+    def forward(k, h, block, panel, ready=None):
+        gather_start(k, h, block)
+        yield
+        gather_wait(k, h)
+        if ready is not None:
+            ready()
+        multiply_start(k, h, panel)
+        yield
+        own = reduce_x(k, h)
+        yield
+        return reduce_z(k, h, own)
+
+    def forward_sent(k, h):
+        wait(r[f"gat{k}"].at[h, 0 : groups[k] - 1], r["gs"].at[k, h])
+        wait(r[f"rx{k}"].at[h], r["xs"].at[k, h])
+        wait(r[f"rz{k}"].at[h], r["zs"].at[k, h])
 
     def spread_x(k, h, row):
         buf = r[f"all{k}"]
-        for d in range(1, nx):
+        for d in x_order:
             send(buf.at[h, row, x], buf.at[h, row, x], r["bxs"].at[k, h], r["bxr"].at[k, h], (leaf, z, lax.rem(x + d, nx)))
 
     def spread_start(k, h, block):
@@ -152,23 +186,55 @@
         result = dot(panel[...], buf[h].reshape(rows, width)).reshape(count, ROWS, width)
         exact[h] = result
         part[h] = result.astype(BF)
+        if is_wide(k):
+            for d in y_order:
+                m = lax.rem(sibling + 2 * d, nleaf)
+                send(part.at[h, m], r["pair"].at[h, d], r["ps"].at[h], r["pr"].at[h, d], (sibling, z, x))
+            return
         for d in range(1, count):
             m = lax.rem(me + d, count)
             send(part.at[h, m], land.at[h, d - 1], r["ls"].at[k, h], r["lr"].at[k, h], (leaf - me + m, z, x))
 
-    def transposed_end(k, h):
-        exact, land = r[f"exact{k}"], r[f"lr{k}"]
+    def transposed_pairs(k, h):
+        exact, pair, land, sums = r[f"exact{k}"], r["pair"], r[f"lr{k}"], r["pairsum"]
+        total = None
+        for d in y_order:
+            m = lax.rem(leaf + 2 * d, nleaf)
+            wait(pair.at[h, d], r["pr"].at[h, d])
+            total = exact[h, m] + pair[h, d].astype(F32)
+            if d:
+                sums[h, d] = total.astype(BF)
+                send(sums.at[h, d], land.at[h, d - 1], r["ls"].at[k, h], r["lr"].at[k, h], (m, z, x))
+        return total
+
+    def transposed_end(k, h, own):
+        land = r[f"lr{k}"]
         wait(land.at[h], r["lr"].at[k, h])
-        total = exact[h, member(k)]
-        for d in range(1, groups[k]):
-            total += land[h, d - 1].astype(F32)
+        total = own
+        for d in range(land.shape[1]):
+            total += land[h, d].astype(F32)
         return total
 
-    def backward_sent(k):
-        for h in range(PARTS):
-            wait(r[f"all{k}"].at[h, 0 : nz - 1, 0], r["bzs"].at[k, h])
-            wait(r[f"all{k}"].at[h, :, 0 : nx - 1], r["bxs"].at[k, h])
-            wait(r[f"lr{k}"].at[h], r["ls"].at[k, h])
+    def backward(k, h, block, panel):
+        spread_start(k, h, block)
+        yield
+        spread_on(k, h)
+        yield
+        transposed_start(k, h, panel)
+        yield
+        if is_wide(k):
+            own = transposed_pairs(k, h)
+            yield
+        else:
+            own = r[f"exact{k}"][h, member(k)]
+        return transposed_end(k, h, own)
+
+    def backward_sent(k, h):
+        wait(r[f"all{k}"].at[h, 0 : nz - 1, 0], r["bzs"].at[k, h])
+        wait(r[f"all{k}"].at[h, :, 0 : nx - 1], r["bxs"].at[k, h])
+        wait(r[f"lr{k}"].at[h], r["ls"].at[k, h])
+        if is_wide(k):
+            wait(r["pair"].at[h], r["ps"].at[h])
 
     def slots(name):
         ids = r["v_w" + name][...]
@@ -196,82 +262,78 @@
     def transpose(name, panel):
         r["t_" + name][...] = panel[...].T
 
-    halves = range(PARTS)
-
-    def forward(k, blocks, panel, after_gather=None, after_x=None):
-        for h in halves:
-            gather_start(k, h, blocks[h])
-        if after_gather is not None:
-            after_gather()
-        for h in halves:
-            multiply_start(k, h, panel)
-        if after_x is not None:
-            after_x()
-        own = [reduce_x(k, h) for h in halves]
-        return [reduce_z(k, h, own[h]) for h in halves]
-
-    def backward(k, blocks, panel, before=None):
-        for h in halves:
-            spread_start(k, h, blocks[h])
-        for h in halves:
-            spread_on(k, h)
-        if before is not None:
-            before()
-        for h in halves:
-            transposed_start(k, h, panel)
-        return [transposed_end(k, h) for h in halves]
+    loaded = set()
 
     def load(*wanted):
         for name in wanted:
-            loads[name].wait()
-
+            if name not in loaded:
+                loads[name].wait()
+                loaded.add(name)
+
+    def solve(h):
+        across = columns(h)
+        first = h == 0
+        total = yield from forward(0, h, r["v_rl"][:, across], r["v_i1"], lambda: load("i1"))
+        solved_leafs = total.astype(BF)
+        total = yield from forward(1, h, solved_leafs, r["p1"])
+        carried = to_targets("1", total)
+        load("rm")
+        block = (r["v_rm"][:, across].astype(F32) - carried[:ROWS]).astype(BF)
+        total = yield from forward(2, h, block, r["v_i2"], lambda: load("i2"))
+        solved_mid = total.astype(BF)
+        total = yield from forward(3, h, solved_mid, r["p2"])
+        load("rr")
+        block = (r["v_rr"][:, across].astype(F32) - carried[ROWS:] - to_targets("2", total)).astype(BF)
+        total = yield from forward(4, h, block, r["v_i3"], lambda: load("i3"))
+
+        total = yield from backward(4, h, total.astype(BF), r["t_i3"])
+        solution_root = total.astype(BF)
+        r["out_r"][:, across] = solution_root
+        total = yield from backward(3, h, dot(r["sel2"][...], solution_root).astype(BF), r["t_p2"])
+        total = yield from backward(2, h, (solved_mid.astype(F32) - total).astype(BF), r["t_i2"])
+        solution_mid = total.astype(BF)
+        r["out_m"][:, across] = solution_mid
+        stacked = jnp.concatenate([solution_mid, solution_root], 0)
+        total = yield from backward(1, h, dot(r["sel1"][...], stacked).astype(BF), r["t_p1"])
+        total = yield from backward(0, h, (solved_leafs.astype(F32) - total).astype(BF), r["t_i1"])
+        r["out_l"][:, across] = total.astype(BF)
+
+    def prepare(number):
+        if number == 1:
+            load("w2", "o2", "f2")
+            slots("2")
+        elif number == 2:
+            load("i1")
+            transpose("i1", r["v_i1"])
+            transpose("p1", r["p1"])
+            transpose("p2", r["p2"])
+        elif number == 4:
+            load("i2", "i3")
+            transpose("i2", r["v_i2"])
+            transpose("i3", r["v_i3"])
+
+    load("w1", "o1", "f1")
+    slots("1")
     load("rl")
     pl.semaphore_wait(barrier, nleaf + nz + nx - 3)
 
-    def prepare_leafs():
-        load("w1", "o1", "f1")
-        slots("1")
-
-    def prepare_mid():
-        load("w2", "o2", "f2")
-        slots("2")
-
-    total = forward(0, [r["v_rl"][:, columns(h)] for h in halves], r["v_i1"], lambda: load("i1"), prepare_leafs)
-    solved_leafs = [t.astype(BF) for t in total]
-    total = forward(1, solved_leafs, r["p1"], None, prepare_mid)
-    carried = [to_targets("1", t) for t in total]
-    load("rm")
-    blocks = [(r["v_rm"][:, columns(h)].astype(F32) - carried[h][:ROWS]).astype(BF) for h in halves]
-    total = forward(2, blocks, r["v_i2"], lambda: load("i2"), lambda: transpose("p1", r["p1"]))
-    solved_mid = [t.astype(BF) for t in total]
-    total = forward(3, solved_mid, r["p2"], None, lambda: transpose("p2", r["p2"]))
-    load("rr")
-    blocks = [
-        (r["v_rr"][:, columns(h)].astype(F32) - carried[h][ROWS:] - to_targets("2", total[h])).astype(BF) for h in halves
-    ]
-    load("i3")
-    total = forward(4, blocks, r["v_i3"], lambda: transpose("i3", r["v_i3"]), lambda: transpose("i2", r["v_i2"]))
-
-    total = backward(4, [t.astype(BF) for t in total], r["t_i3"], lambda: transpose("i1", r["v_i1"]))
-    solution_root = [t.astype(BF) for t in total]
-    for h in halves:
-        r["out_r"][:, columns(h)] = solution_root[h]
-    total = backward(3, [dot(r["sel2"][...], solution_root[h]).astype(BF) for h in halves], r["t_p2"])
-    rest = [(solved_mid[h].astype(F32) - total[h]).astype(BF) for h in halves]
-    total = backward(2, rest, r["t_i2"])
-    solution_mid = [t.astype(BF) for t in total]
-    for h in halves:
-        r["out_m"][:, columns(h)] = solution_mid[h]
-    stacked = [jnp.concatenate([solution_mid[h], solution_root[h]], 0) for h in halves]
-    total = backward(1, [dot(r["sel1"][...], stacked[h]).astype(BF) for h in halves], r["t_p1"])
-    rest = [(solved_leafs[h].astype(F32) - total[h]).astype(BF) for h in halves]
-    total = backward(0, rest, r["t_i1"])
-    for h in halves:
-        r["out_l"][:, columns(h)] = total[h].astype(BF)
+    chains = [solve(h) for h in range(PARTS)]
+    for h, chain in enumerate(chains):
+        for _ in range(LEAD * (PARTS - 1 - h)):
+            next(chain)
+    running = list(chains)
+    number = 0
+    while running:
+        for chain in list(running):
+            if next(chain, running) is running:
+                running.remove(chain)
+        prepare(number)
+        number += 1
 
     for k in range(5):
-        forward_sent(k)
-        backward_sent(k)
+        for h in range(PARTS):
+            forward_sent(k, h)
+            backward_sent(k, h)
 
 
 def shards(
@@ -343,7 +405,12 @@
         keep(f"all{k}", (PARTS, nz, nx, ROWS, width))
         keep(f"part{k}", (PARTS, count, ROWS, width))
         keep(f"exact{k}", (PARTS, count, ROWS, width), F32)
-        keep(f"lr{k}", (PARTS, count - 1, ROWS, width))
+        keep(f"lr{k}", (PARTS, (count // 2 if count == nleaf else count) - 1, ROWS, width))
+    keep("pair", (PARTS, nleaf // 2, ROWS, width))
+    keep("pairsum", (PARTS, nleaf // 2, ROWS, width))
+    semaphores("gyr", (PARTS, nleaf // 2 - 1))
+    semaphores("ps", (PARTS,))
+    semaphores("pr", (PARTS, nleaf // 2))
     for name in ("gs", "gr", "xs", "zs", "zr", "bzs", "bxs", "bxr", "ls", "lr"):
         semaphores(name, (5, PARTS))
     semaphores("xr", (5, PARTS, nz // CHUNK))
@@ -356,7 +423,7 @@
         in_specs=[pl.BlockSpec(memory_space=pl.ANY)] * len(operands),
         out_specs=[pl.BlockSpec(memory_space=pltpu.VMEM)] * 3,
         scratch_shapes=scratch,
-        compiler_params=pltpu.CompilerParams(collective_id=0, has_side_effects=True, vmem_limit_bytes=50 * 2**20),
+        compiler_params=pltpu.CompilerParams(collective_id=0, has_side_effects=True, vmem_limit_bytes=63 * 2**20),
         cost_estimate=pl.CostEstimate(flops=1_200_000_000, bytes_accessed=2_400_000, transcendentals=0),
         name="triangular_solve",
     )(*operands.values())

time: 188 us -> 154 us (0.82)
  Pallas kernels: 175 us -> 150 us
  local copies, waits for them, and re-layouts: 11.8 us -> 2.66 us
    pallas_call x1, Pallas kernels: 175 us -> 150 us  [shards(): pl.pallas_call(functools.partial(kernel, (tuple(names), groups, nz, nx)),...]
    unnamed x27 -> x7, local copies, waits for them, and re-layouts: 11.8 us -> 2.66 us
where the time goes in v2:
time: 154 us; the launch traced here: 153 us
  Pallas kernels  150 us (97%)
  local copies, waits for them, and re-layouts  2.66 us (2%)
    pallas_call x1, Pallas kernels, shards(): pl.pallas_call(functools.partial(kernel, (tuple(names), groups, nz, nx)),...  150 us

profile of v2, /device:TPU:1, one launch (start us, length us, event | category | flops | bytes accessed | tf_op | source)
XLA Modules:
  0.0 153.3 jit_solution(17068123821342865902)
XLA Ops:
  0.6 150.0 %triangular_solve.1 = (bf16[32,256]{1,0:T(8,128)(2,1)}, bf16[32,256]{1,0:T(8,128)(2,1)}, bf16[32,256]{1,0:T(8,128)(2,1)}) custom-call(bf16[32,256]{1,0:T(8,128)(2,1)} %refs_0_.1, bf16[32,256]{1,0:T(8,128)(2,1)} %refs_1_.1, bf16[32,256]{1,0:T(8,128)(2,1)} %refs_2_.1, bf16[1024,128]{1,0:T(8,128)(2,1)} %bitcast.11, bf16[1024,256]{1,0:T(8,128)(2,1)} %bitcast.10, ...), custom_call_target="tpu_custom_call" | custom-call | flops 1200000000 | bytes 2400000 | tf_op jit(solution)/shard_map/triangular_solve/pallas_call | solution.py:420
  150.6 0.0 copy-start.1
  150.6 1.3 copy.18
  152.0 0.0 copy-done.1
  152.0 0.0 copy-start
  152.0 0.6 copy.19
  152.6 0.1 copy-done
  152.7 0.6 copy.20
Async XLA Ops:
  150.6 1.3 copy-start.1
  152.0 0.7 copy-start

commit v3 on v2

--- a/solution.py
+++ b/solution.py
@@ -13,7 +13,8 @@
 ROWS = 32
 NRHS = 256
 PARTS = 2
-CHUNK = 1
+CHUNK = 2
+Y_FAR = 3
 LEAD = 1
 
 
@@ -47,22 +48,26 @@
     rows = nz * nx * ROWS
     nleaf = groups[4]
     y_order = z_order(nleaf // 2)
+    y_far = y_order[:Y_FAR]
     x_order = z_order(nx)[:-1]
     sibling = leaf + 1 - 2 * lax.rem(leaf, 2)
+
+    barrier = pltpu.get_barrier_semaphore()
+    for d in z_order(nz)[:-1]:
+        pl.semaphore_signal(barrier, inc=1, device_id=(leaf, lax.rem(z + d, nz), x), device_id_type=MESH)
+    for d in y_order[:-1]:
+        for core in range(2):
+            there = lax.rem(leaf - lax.rem(leaf, 2) + 2 * d + core, nleaf)
+            pl.semaphore_signal(barrier, inc=1, device_id=(there, z, x), device_id_type=MESH)
+    for d in range(1, nx):
+        pl.semaphore_signal(barrier, inc=1, device_id=(leaf, z, lax.rem(x + d, nx)), device_id_type=MESH)
+    pl.semaphore_signal(barrier, inc=1, device_id=(sibling, z, x), device_id_type=MESH)
 
     loads = {}
     for number, name in enumerate(("rl", "i1", "w1", "o1", "f1", "rm", "i2", "rr", "w2", "o2", "f2", "i3")):
         loads[name] = pltpu.make_async_copy(r["in_" + name], r["v_" + name], r["load"].at[number])
         loads[name].start()
 
-    barrier = pltpu.get_barrier_semaphore()
-    for d in range(1, nleaf):
-        pl.semaphore_signal(barrier, inc=1, device_id=(lax.rem(leaf + d, nleaf), z, x), device_id_type=MESH)
-    for d in range(1, nz):
-        pl.semaphore_signal(barrier, inc=1, device_id=(leaf, lax.rem(z + d, nz), x), device_id_type=MESH)
-    for d in range(1, nx):
-        pl.semaphore_signal(barrier, inc=1, device_id=(leaf, z, lax.rem(x + d, nx)), device_id_type=MESH)
-
     def send(source, target, send_sem, recv_sem, where):
         pltpu.make_async_remote_copy(
             src_ref=source, dst_ref=target, send_sem=send_sem, recv_sem=recv_sem, device_id=where, device_id_type=MESH
@@ -76,6 +81,17 @@
 
     def columns(h):
         return slice(h * width, (h + 1) * width)
+
+    def flipped(me, bits):
+        there, bit = me, 1
+        while bit <= bits:
+            if bits & bit:
+                there = there + bit * (1 - 2 * lax.rem(me // bit, 2))
+            bit *= 2
+        return there
+
+    def flips(count):
+        return sorted(range(1, count), reverse=True)
 
     def is_wide(k):
         return groups[k] == nleaf
@@ -87,11 +103,12 @@
             own = buf.at[h, me]
             for d in y_order[:-1]:
                 send(own, own, r["gs"].at[k, h], r["gyr"].at[h, d - 1], (lax.rem(leaf + 2 * d, nleaf), z, x))
+                if d in y_far:
+                    send(own, own, r["gs"].at[k, h], r["gr"].at[k, h], (lax.rem(sibling + 2 * d, nleaf), z, x))
             send(own, own, r["gs"].at[k, h], r["gr"].at[k, h], (sibling, z, x))
             return
-        for d in range(1, count):
-            there = leaf - me + lax.rem(me + d, count)
-            send(buf.at[h, me], buf.at[h, me], r["gs"].at[k, h], r["gr"].at[k, h], (there, z, x))
+        for d in flips(count):
+            send(buf.at[h, me], buf.at[h, me], r["gs"].at[k, h], r["gr"].at[k, h], (leaf - me + flipped(me, d), z, x))
 
     def gather_wait(k, h):
         count, buf = groups[k], r[f"gat{k}"]
@@ -99,7 +116,8 @@
             for d in reversed(y_order[:-1]):
                 m = lax.rem(leaf + nleaf - 2 * d, nleaf)
                 wait(buf.at[h, m], r["gyr"].at[h, d - 1])
-                send(buf.at[h, m], buf.at[h, m], r["gs"].at[k, h], r["gr"].at[k, h], (sibling, z, x))
+                if d not in y_far:
+                    send(buf.at[h, m], buf.at[h, m], r["gs"].at[k, h], r["gr"].at[k, h], (sibling, z, x))
             wait(buf.at[h, 0 : nleaf // 2], r["gr"].at[k, h])
         else:
             wait(buf.at[h, 0 : count - 1], r["gr"].at[k, h])
@@ -146,6 +164,8 @@
 
     def forward(k, h, block, panel, ready=None):
         gather_start(k, h, block)
+        if k:
+            forward_sent(k - 1, h)
         yield
         gather_wait(k, h)
         if ready is not None:
@@ -191,8 +211,8 @@
                 m = lax.rem(sibling + 2 * d, nleaf)
                 send(part.at[h, m], r["pair"].at[h, d], r["ps"].at[h], r["pr"].at[h, d], (sibling, z, x))
             return
-        for d in range(1, count):
-            m = lax.rem(me + d, count)
+        for d in flips(count):
+            m = flipped(me, d)
             send(part.at[h, m], land.at[h, d - 1], r["ls"].at[k, h], r["lr"].at[k, h], (leaf - me + m, z, x))
 
     def transposed_pairs(k, h):
@@ -217,6 +237,10 @@
 
     def backward(k, h, block, panel):
         spread_start(k, h, block)
+        if k == 4:
+            forward_sent(4, h)
+        else:
+            backward_sent(k + 1, h)
         yield
         spread_on(k, h)
         yield
@@ -299,7 +323,10 @@
         r["out_l"][:, across] = total.astype(BF)
 
     def prepare(number):
-        if number == 1:
+        if number == 0:
+            load("w1", "o1", "f1")
+            slots("1")
+        elif number == 1:
             load("w2", "o2", "f2")
             slots("2")
         elif number == 2:
@@ -312,8 +339,6 @@
             transpose("i2", r["v_i2"])
             transpose("i3", r["v_i3"])
 
-    load("w1", "o1", "f1")
-    slots("1")
     load("rl")
     pl.semaphore_wait(barrier, nleaf + nz + nx - 3)
 
@@ -330,10 +355,8 @@
         prepare(number)
         number += 1
 
-    for k in range(5):
-        for h in range(PARTS):
-            forward_sent(k, h)
-            backward_sent(k, h)
+    for h in range(PARTS):
+        backward_sent(0, h)
 
 
 def shards(

time: 154 us -> 151 us (0.981)
  Pallas kernels: 150 us -> 148 us
    pallas_call x1, Pallas kernels: 150 us -> 148 us  [shards(): pl.pallas_call(functools.partial(kernel, (tuple(names), groups, nz, nx)),...]
where the time goes in v3:
time: 151 us
  Pallas kernels  148 us (98%)
  local copies, waits for them, and re-layouts  2.66 us (2%)
    pallas_call x1, Pallas kernels, shards(): pl.pallas_call(functools.partial(kernel, (tuple(names), groups, nz, nx)),...  148 us

profile of v3, /device:TPU:1, one launch (start us, length us, event | category | flops | bytes accessed | tf_op | source)
XLA Modules:
  0.0 151.1 jit_solution(11865022809254071857)
XLA Ops:
  0.6 147.8 %triangular_solve.1 = (bf16[32,256]{1,0:T(8,128)(2,1)}, bf16[32,256]{1,0:T(8,128)(2,1)}, bf16[32,256]{1,0:T(8,128)(2,1)}) custom-call(bf16[32,256]{1,0:T(8,128)(2,1)} %refs_0_.1, bf16[32,256]{1,0:T(8,128)(2,1)} %refs_1_.1, bf16[32,256]{1,0:T(8,128)(2,1)} %refs_2_.1, bf16[1024,128]{1,0:T(8,128)(2,1)} %bitcast.11, bf16[1024,256]{1,0:T(8,128)(2,1)} %bitcast.10, ...), custom_call_target="tpu_custom_call" | custom-call | flops 1200000000 | bytes 2400000 | tf_op jit(solution)/shard_map/triangular_solve/pallas_call | solution.py:443
  148.4 0.0 copy-start.1
  148.4 1.3 copy.18
  149.7 0.0 copy-done.1
  149.7 0.0 copy-start
  149.7 0.6 copy.19
  150.4 0.1 copy-done
  150.5 0.6 copy.20
Async XLA Ops:
  148.4 1.3 copy-start.1
  149.7 0.7 copy-start

commit v4 on v3

--- a/solution.py
+++ b/solution.py
@@ -312,15 +312,15 @@
 
         total = yield from backward(4, h, total.astype(BF), r["t_i3"])
         solution_root = total.astype(BF)
-        r["out_r"][:, across] = solution_root
+        r["out"][2, :, across] = solution_root
         total = yield from backward(3, h, dot(r["sel2"][...], solution_root).astype(BF), r["t_p2"])
         total = yield from backward(2, h, (solved_mid.astype(F32) - total).astype(BF), r["t_i2"])
         solution_mid = total.astype(BF)
-        r["out_m"][:, across] = solution_mid
+        r["out"][1, :, across] = solution_mid
         stacked = jnp.concatenate([solution_mid, solution_root], 0)
         total = yield from backward(1, h, dot(r["sel1"][...], stacked).astype(BF), r["t_p1"])
         total = yield from backward(0, h, (solved_leafs.astype(F32) - total).astype(BF), r["t_i1"])
-        r["out_l"][:, across] = total.astype(BF)
+        r["out"][0, :, across] = total.astype(BF)
 
     def prepare(number):
         if number == 0:
@@ -397,7 +397,7 @@
         "f2": offset_mid.reshape(1, -1),
     }
     places = off_leafs.shape[0]
-    names = ["in_" + name for name in operands] + ["out_l", "out_m", "out_r"]
+    names = ["in_" + name for name in operands] + ["out"]
     scratch = []
 
     def keep(name, shape, dtype=BF):
@@ -439,17 +439,18 @@
     semaphores("xr", (5, PARTS, nz // CHUNK))
     semaphores("bzr", (5, PARTS, nz - 1))
 
-    block = jax.ShapeDtypeStruct(rhs_leafs.shape, rhs_leafs.dtype)
-    return pl.pallas_call(
+    block = jax.ShapeDtypeStruct((3, *rhs_leafs.shape), BF)
+    solved = pl.pallas_call(
         functools.partial(kernel, (tuple(names), groups, nz, nx)),
-        out_shape=(block, block, block),
+        out_shape=block,
         in_specs=[pl.BlockSpec(memory_space=pl.ANY)] * len(operands),
-        out_specs=[pl.BlockSpec(memory_space=pltpu.VMEM)] * 3,
+        out_specs=pl.BlockSpec(memory_space=pltpu.VMEM),
         scratch_shapes=scratch,
         compiler_params=pltpu.CompilerParams(collective_id=0, has_side_effects=True, vmem_limit_bytes=63 * 2**20),
         cost_estimate=pl.CostEstimate(flops=1_200_000_000, bytes_accessed=2_400_000, transcendentals=0),
         name="triangular_solve",
     )(*operands.values())
+    return tuple(solved[level].astype(BF) for level in range(3))
 
 
 def solution(mesh):

time: 151 us -> 150 us (level)
    unnamed x7 -> x0, local copies, waits for them, and re-layouts: 2.66 us -> none
where the time goes in v4:
time: 150 us
  Pallas kernels  148 us (99%)
    pallas_call x1, Pallas kernels, shards(): pl.pallas_call(functools.partial(kernel, (tuple(names), groups, nz, nx)),...  148 us

profile of v4, /device:TPU:1, one launch (start us, length us, event | category | flops | bytes accessed | tf_op | source)
XLA Modules:
  0.0 150.1 jit_solution(9480144213503928599)
XLA Ops:
  0.6 148.0 %triangular_solve.1 = bf16[3,32,256]{2,1,0:T(8,128)(2,1)} custom-call(bf16[32,256]{1,0:T(8,128)(2,1)} %refs_0_.1, bf16[32,256]{1,0:T(8,128)(2,1)} %refs_1_.1, bf16[32,256]{1,0:T(8,128)(2,1)} %refs_2_.1, bf16[1024,128]{1,0:T(8,128)(2,1)} %bitcast.17, bf16[1024,256]{1,0:T(8,128)(2,1)} %bitcast.16, bf16[1024,512]{1,0:T(8,128)(2,1)} %bitcast.15, ...), custom_call_target="tpu_custom_call" | custom-call | flops 1200000000 | bytes 2400000 | tf_op jit(solution)/shard_map/triangular_solve/pallas_call | solution.py:443
  148.7 1.4 slice_bitcast_fusion
